TPU v7x, 32 devices: a whole 2x2x4 slice. The times are simulated.
32 devices in a mesh: groups: 2 (over y), tiles: 4 (over z), feat: 2 (over x), rep: 2 (over core).
Axes of the slice: x: 2, y: 2, z: 4, core: 2. Of those that a mesh axis runs over, the one named last changes fastest.
Arguments:
- points: bfloat16 [65536, 512], P(('groups', 'tiles', 'rep')), parts along dimension 0, may hold values from -6 to 6
- dest_tile: int32 [65536, 1], P(('groups', 'tiles', 'rep')), parts along dimension 0, may hold values from 0 to 3; in each aligned block of 4096 rows (0 to 4095, 4096 to 8191, ...) at most 3072 rows name the same one
- member: int32 [65536], P(('groups', 'tiles', 'rep')), parts along dimension 0, may hold values from 0 to 255
- w_point: bfloat16 [512, 512], P(None, 'feat'), may hold values from -0.25 to 0.25
- ln_gain: float32 [512], replicated, may hold values from 0.5 to 1.5
- w_qkv: bfloat16 [3, 512, 512], P(None, None, 'feat'), may hold values from -0.25 to 0.25
- temper: float32 [8], P('feat'), may hold values from 4 to 12
- w_out: bfloat16 [512, 512], P('feat'), may hold values from -0.25 to 0.25
- adjacency: int32 [16, 4], P(('groups', 'tiles', 'rep')), parts along dimension 0, may hold values 0 or 1
Outputs:
- states: bfloat16 [2048, 512], P(('groups', 'tiles', 'rep'), 'feat'), parts along dimension 0
There are 2 independent parts, one for each index of `groups`. A program takes and returns all parts, laid end to end along the dimension named above; an argument that names none is the same for every part. Nothing has to cross between parts.
Inputs may be any that keep to these rules, and one draw needn't show every extreme that they name: `dest_tile`: no more than 3072 rows of one device name one tile; in every draw some device sends exactly 3072 rows to some tile.
All inputs are finite; a program needn't handle non-finite values. No bound on the sum of `adjacency` on one device may be relied on, other than what follows from the above.
Results may differ from a plain program's by a relative error of at most 0.008.
Values may be sent and summed in bfloat16 or wider, within the bound.
A program may use at most 64 MiB of HBM per device.

v0:
```python
import jax
import jax.numpy as jnp
from jax import lax
from jax.sharding import PartitionSpec as P

S_BLK = 128
REACH = 2


def from_behind(block, axis, distance):
    devices = range(lax.axis_size(axis))
    route = [(i - distance, i) for i in devices if i - distance in devices]
    return lax.ppermute(block, axis, route)


def unit_heads(proj, heads):
    shaped = proj.reshape(proj.shape[0], heads, -1)
    return shaped * lax.rsqrt(jnp.sum(shaped * shaped, axis=-1, keepdims=True) + 1e-06)


def bucket_rows(hidden, bucket, local_id, buckets, capacity):
    onehot_rank = (bucket[:, None] == jnp.arange(buckets, dtype=jnp.int32)[None, :]).astype(
        jnp.int32
    )
    position = jnp.sum(jnp.cumsum(onehot_rank, axis=0) * onehot_rank, axis=1) - 1
    slot_of = bucket * capacity + position
    width = hidden.shape[1]
    packed = jnp.zeros((buckets * capacity, width), hidden.dtype).at[slot_of].set(hidden)
    labels = jnp.full((buckets * capacity,), -1, jnp.int32).at[slot_of].set(local_id)
    return (packed.reshape(buckets, capacity, width), labels.reshape(buckets, capacity))


def pool_rows(packed, labels, owners):
    flat = packed.reshape(-1, packed.shape[-1])
    flat_labels = labels.reshape(-1)
    onehot = (jnp.arange(owners, dtype=jnp.int32)[:, None] == flat_labels[None, :]).astype(
        jnp.bfloat16
    )
    sums = jnp.dot(onehot, flat, preferred_element_type=jnp.float32)
    counts = jnp.sum(onehot, axis=1, dtype=jnp.float32)
    return (sums, counts)


def body(points, dest_tile, member, w_point, ln_gain, w_qkv, temper, w_out, adjacency):
    tiles = lax.axis_size("tiles")
    reps = lax.axis_size("rep")
    blocks = tiles * reps
    rows_dev = points.shape[0]
    capacity = 3 * rows_dev // tiles
    hidden = jax.nn.gelu(jnp.dot(points, w_point, preferred_element_type=jnp.float32)).astype(
        jnp.bfloat16
    )
    target = dest_tile[:, 0]
    packed, labels = bucket_rows(hidden, target, member, tiles, capacity)
    packed, labels = (
        lax.all_to_all(packed, "tiles", split_axis=0, concat_axis=0, tiled=True),
        lax.all_to_all(labels, "tiles", split_axis=0, concat_axis=0, tiled=True),
    )
    sums, counts = pool_rows(packed, labels, reps * S_BLK)
    sums, counts = (
        lax.psum_scatter(sums, "rep", scatter_dimension=0, tiled=True),
        lax.psum_scatter(counts, "rep", scatter_dimension=0, tiled=True),
    )
    pooled = (sums / jnp.maximum(counts, 1.0)[:, None]).astype(jnp.bfloat16)
    full_rows = lax.all_gather(pooled, "feat", axis=1, tiled=True)
    lifted = full_rows.astype(jnp.float32)
    mean = jnp.mean(lifted, axis=1, keepdims=True)
    var = jnp.mean((lifted - mean) ** 2, axis=1, keepdims=True)
    normed = ((lifted - mean) * lax.rsqrt(var + 1e-05) * ln_gain).astype(jnp.bfloat16)
    share = w_qkv.shape[2]
    heads_here = temper.shape[0]
    proj = jnp.einsum("sd,ide->ise", normed, w_qkv, preferred_element_type=jnp.float32)
    query = unit_heads(proj[0], heads_here).astype(jnp.bfloat16)
    key_flat = unit_heads(proj[1], heads_here).astype(jnp.bfloat16).reshape(S_BLK, share)
    value_flat = proj[2].astype(jnp.bfloat16)
    paired = jnp.stack([key_flat, value_flat], axis=1)
    offsets = list(range(-REACH, 0)) + list(range(1, REACH + 1))
    rep_index = lax.axis_index("rep")
    block_index = lax.axis_index("tiles") * reps + rep_index
    neighbours = []
    for offset in offsets:
        neighbours.append(from_behind(paired, ("tiles", "rep"), -offset))
    columns = [jnp.ones((), jnp.float32)]
    for column, offset in enumerate(offsets):
        inside = (
            (block_index + offset >= 0)
            & (block_index + offset < blocks)
            & (adjacency[0, column] == 1)
        )
        columns.append(inside.astype(jnp.float32))
    keymask = jnp.repeat(jnp.stack(columns), S_BLK)
    every = jnp.concatenate([paired] + neighbours, axis=0)
    keys = every[:, 0].reshape(every.shape[0], heads_here, -1)
    values = every[:, 1].reshape(every.shape[0], heads_here, -1)
    scores = jnp.einsum("qhd,khd->hqk", query, keys, preferred_element_type=jnp.float32)
    scores = scores * temper[:, None, None]
    expd = jnp.exp(scores) * keymask[None, None, :]
    probs = (expd / jnp.sum(expd, axis=-1, keepdims=True)).astype(jnp.bfloat16)
    attended = jnp.einsum("hqk,khd->qhd", probs, values, preferred_element_type=jnp.float32)
    attended = attended.astype(jnp.bfloat16).reshape(S_BLK, share)
    partial_out = jnp.dot(attended, w_out, preferred_element_type=jnp.float32)
    summed = lax.psum_scatter(partial_out, "feat", scatter_dimension=1, tiled=True)
    return (pooled.astype(jnp.float32) + summed).astype(jnp.bfloat16)


def solution(mesh):
    return jax.shard_map(
        body,
        mesh=mesh,
        in_specs=(
            P(("groups", "tiles", "rep"), None),
            P(("groups", "tiles", "rep"), None),
            P(("groups", "tiles", "rep")),
            P(None, "feat"),
            P(),
            P(None, None, "feat"),
            P("feat"),
            P("feat", None),
            P(("groups", "tiles", "rep"), None),
        ),
        out_specs=P(("groups", "tiles", "rep"), "feat"),
        check_vma=False,
    )
```

profile of v0, /device:TPU:0, one launch (start us, length us, event | category | flops | bytes accessed | tf_op | source)
XLA Modules:
  0.0 263.2 jit_solution(11526518464585433747)
XLA Ops:
  6.5 0.8 fusion.36
  7.3 1.1 reduce-window.6
  9.0 0.8 fusion.34
  10.6 16.3 %scatter_custom_fusion = s32[12288]{0:T(1024)} fusion(s32[4096]{0:T(1024)S(1)} %bitcast.75, s32[4096]{0:T(1024)} %param.11, s32[]{:T(128)} %constant.22.clone.1), kind=kCustom, calls=%fused_computation.60 | custom fusion | bytes 49664 | tf_op jit(solution)/shard_map/scatter | solution.py:29
  26.9 6.3 %all-to-all-start = ((s32[4,1,3072]{2,1,0:T(1,128)}), s32[4,1,3072]{2,1,0:T(1,128)S(1)}, u32[]{:S(2)}, u32[]{:S(2)}) async-start(s32[4,1,3072]{2,1,0:T(1,128)} %bitcast.5), calls=%async_computation | async-start | bytes 98304 | tf_op jit(solution)/shard_map/all_to_all | solution.py:57
  33.2 5.4 %fusion.43 = f32[4096,256]{1,0:T(8,128)} fusion(bf16[4096,512]{1,0:T(8,128)(2,1)} %param.9, bf16[512,256]{1,0:T(8,128)(2,1)} %param.12), kind=kOutput, calls=%fused_computation.78 | convolution fusion | flops 1073741824 | bytes 8650752 | tf_op jit(solution)/shard_map/dot_general | solution.py:50
  38.6 23.1 %scatter_custom_fusion.1 = bf16[12288,256]{1,0:T(8,128)(2,1)} fusion(s32[4096]{0:T(1024)S(1)} %bitcast.76, bf16[]{:T(256)} %constant.14.clone.1, f32[4096,256]{1,0:T(8,128)} %fusion.43, f32[]{:T(128)} %constant.18.clone.1, f32[]{:T(128)} %constant.17.clone.1, f32[]{:T(128)} %constant.16.clone.1, f32[]{:T(128)} %constant.15.clone.1), kind=kCustom, calls=%fused_computation.16 | custom fusion | flops 9437184 | bytes 10485778 | tf_op jit(solution)/shard_map/scatter | solution.py:28
  61.7 5.4 %all-to-all-start.1 = ((bf16[4,3072,256]{2,1,0:T(8,128)(2,1)}), bf16[4,3072,256]{2,1,0:T(8,128)(2,1)}, u32[]{:S(2)}, u32[]{:S(2)}) async-start(bf16[4,3072,256]{2,1,0:T(8,128)(2,1)} %bitcast.62), calls=%async_computation.1 | async-start | bytes 12582912 | tf_op jit(solution)/shard_map/all_to_all | solution.py:56
  71.9 133.4 %all-to-all-done.1 = bf16[4,3072,256]{2,1,0:T(8,128)(2,1)} async-done(((bf16[4,3072,256]{2,1,0:T(8,128)(2,1)}), bf16[4,3072,256]{2,1,0:T(8,128)(2,1)}, u32[]{:S(2)}, u32[]{:S(2)}) %all-to-all-start.1) | async-done | bytes 6291488 | tf_op jit(solution)/shard_map/all_to_all | solution.py:56
  205.2 5.3 %fusion.1 = f32[256,256]{1,0:T(8,128)} fusion(bf16[12288,256]{1,0:T(8,128)(2,1)} %bitcast.8, s32[12288]{0:T(1024)S(1)} %bitcast.69), kind=kOutput, calls=%fused_computation.5 | convolution fusion | flops 1613758464 | bytes 6602752 | tf_op jit(solution)/shard_map/dot_general | solution.py:39
  210.9 2.1 convert_reduce_fusion
  213.0 2.5 all-reduce
  215.5 2.0 reduce-scatter.3.cloned.1.call-done
  217.5 1.0 divide_convert_fusion.1
  218.5 4.9 %all_gather.3 = bf16[128,512]{1,0:T(8,128)(2,1)S(1)} all-gather(bf16[128,256]{1,0:T(8,128)(2,1)S(1)} %divide_convert_fusion.1), channel_id=1, replica_groups=mesh['groups'=2,'tiles'=4,'feat'=2,'rep'=2] {'feat'}, dimensions={1}, use_global_device_ids=true | all-gather | bytes 196608 | tf_op jit(solution)/shard_map/all_gather | solution.py:65
  224.4 3.7 %collective-permute-start = (bf16[128,2,256]{2,0,1:T(8,128)(2,1)S(1)}, bf16[128,2,256]{2,0,1:T(8,128)(2,1)S(1)}, u32[]{:S(2)}, u32[]{:S(2)}) collective-permute-start(bf16[128,2,256]{2,0,1:T(8,128)(2,1)S(1)} %get-tuple-element.9), channel_id=1, source_target_pairs={{0,4},{1,5},{4,8},{5,9},{8,12},{9,13},{2,6},{3,7},{6,10},{7,11},{1... | collective-permute-start | bytes 393224 | tf_op jit(solution)/shard_map/ppermute | solution.py:13
  228.1 1.3 collective-permute-start.1
  229.5 1.3 collective-permute-start.2
  230.8 1.3 collective-permute-start.3
  232.3 2.1 collective-permute-done.2
  234.4 6.5 %collective-permute-done.3 = bf16[128,2,256]{2,0,1:T(8,128)(2,1)S(1)} collective-permute-done((bf16[128,2,256]{2,0,1:T(8,128)(2,1)S(1)}, bf16[128,2,256]{2,0,1:T(8,128)(2,1)S(1)}, u32[]{:S(2)}, u32[]{:S(2)}) %collective-permute-start.3) | collective-permute-done | bytes 131104 | tf_op jit(solution)/shard_map/ppermute | solution.py:13
  242.3 0.9 fusion.44
  243.3 11.5 %reduce-scatter.5.cloned.1.call-done = f32[128,256]{1,0:T(8,128)} async-done(((f32[128,512]{1,0:T(8,128)}), f32[128,256]{1,0:T(8,128)}) %reduce-scatter.5.cloned.1.call-update) | async-done | bytes 131088 | tf_op jit(solution)/shard_map/reduce_scatter | solution.py:102
  254.7 1.6 add_convert_fusion
  (58 shorter events, 5.5 us)
Async XLA Ops:
  6.5 217.2 %copy-start = (bf16[3,512,256]{2,1,0:T(8,128)(2,1)S(1)}, bf16[3,512,256]{2,1,0:T(8,128)(2,1)}, u32[]{:S(2)}) copy-start(bf16[3,512,256]{2,1,0:T(8,128)(2,1)} %param.14) | copy-start | bytes 2359300
  26.9 34.8 %all-to-all-start = ((s32[4,1,3072]{2,1,0:T(1,128)}), s32[4,1,3072]{2,1,0:T(1,128)S(1)}, u32[]{:S(2)}, u32[]{:S(2)}) async-start(s32[4,1,3072]{2,1,0:T(1,128)} %bitcast.5), calls=%async_computation | async-start | bytes 98304 | tf_op jit(solution)/shard_map/all_to_all | solution.py:57
  61.7 5.5 %copy-start.3 = (s32[1,4]{1,0:T(1,128)S(1)}, s32[1,4]{1,0:T(1,128)}, u32[]{:S(2)}) copy-start(s32[1,4]{1,0:T(1,128)} %param.17) | copy-start | bytes 52
  61.7 8.9 %copy-start.6 = (u32[32]{0:T(128)S(1)}, u32[32]{0:T(128)}, u32[]{:S(2)}) copy-start(u32[32]{0:T(128)} %constant.65) | copy-start | bytes 388
  61.7 143.5 %all-to-all-start.1 = ((bf16[4,3072,256]{2,1,0:T(8,128)(2,1)}), bf16[4,3072,256]{2,1,0:T(8,128)(2,1)}, u32[]{:S(2)}, u32[]{:S(2)}) async-start(bf16[4,3072,256]{2,1,0:T(8,128)(2,1)} %bitcast.62), calls=%async_computation.1 | async-start | bytes 12582912 | tf_op jit(solution)/shard_map/all_to_all | solution.py:56
  67.1 150.4 %reduce-scatter.3.cloned.1.call-start = ((), (), s32[]{:S(2)}) async-start(), calls=%async_computation.4 | async-start | bytes 393216 | tf_op jit(solution)/shard_map/reduce_scatter | solution.py:61
  205.2 18.5 %copy-start.4 = (f32[512]{0:T(512)S(1)}, f32[512]{0:T(512)}, u32[]{:S(2)}) copy-start(f32[512]{0:T(512)} %param.13) | copy-start | bytes 6148
  210.5 30.9 %copy-start.5 = (f32[4]{0:T(128)S(1)}, f32[4]{0:T(128)}, u32[]{:S(2)}) copy-start(f32[4]{0:T(128)} %param.15) | copy-start | bytes 52
  210.6 44.2 %reduce-scatter.5.cloned.1.call-start = ((), (), s32[]{:S(2)}) async-start(), calls=%async_computation.5 | async-start | bytes 393216 | tf_op jit(solution)/shard_map/reduce_scatter | solution.py:102
  224.4 7.7 %collective-permute-start = (bf16[128,2,256]{2,0,1:T(8,128)(2,1)S(1)}, bf16[128,2,256]{2,0,1:T(8,128)(2,1)S(1)}, u32[]{:S(2)}, u32[]{:S(2)}) collective-permute-start(bf16[128,2,256]{2,0,1:T(8,128)(2,1)S(1)} %get-tuple-element.9), channel_id=1, source_target_pairs={{0,4},{1,5},{4,8},{5,9},{8,12},{9,13},{2,6},{3,7},{6,10},{7,11},{1... | collective-permute-start | bytes 393224 | tf_op jit(solution)/shard_map/ppermute | solution.py:13
  228.1 4.1 %collective-permute-start.1 = (bf16[128,2,256]{2,0,1:T(8,128)(2,1)S(1)}, bf16[128,2,256]{2,0,1:T(8,128)(2,1)S(1)}, u32[]{:S(2)}, u32[]{:S(2)}) collective-permute-start(bf16[128,2,256]{2,0,1:T(8,128)(2,1)S(1)} %get-tuple-element.9), channel_id=1, source_target_pairs={{0,1},{1,4},{4,5},{5,8},{8,9},{9,12},{12,13},{2,3},{3,6},{6,7},{7,... | collective-permute-start | bytes 393224 | tf_op jit(solution)/shard_map/ppermute | solution.py:13
  229.5 4.9 %collective-permute-start.2 = (bf16[128,2,256]{2,0,1:T(8,128)(2,1)S(1)}, bf16[128,2,256]{2,0,1:T(8,128)(2,1)S(1)}, u32[]{:S(2)}, u32[]{:S(2)}) collective-permute-start(bf16[128,2,256]{2,0,1:T(8,128)(2,1)S(1)} %get-tuple-element.9), channel_id=1, source_target_pairs={{1,0},{4,1},{5,4},{8,5},{9,8},{12,9},{13,12},{3,2},{6,3},{7,6},{10... | collective-permute-start | bytes 393224 | tf_op jit(solution)/shard_map/ppermute | solution.py:13
  230.8 10.2 %collective-permute-start.3 = (bf16[128,2,256]{2,0,1:T(8,128)(2,1)S(1)}, bf16[128,2,256]{2,0,1:T(8,128)(2,1)S(1)}, u32[]{:S(2)}, u32[]{:S(2)}) collective-permute-start(bf16[128,2,256]{2,0,1:T(8,128)(2,1)S(1)} %get-tuple-element.9), channel_id=1, source_target_pairs={{4,0},{5,1},{8,4},{9,5},{12,8},{13,9},{6,2},{7,3},{10,6},{11,7},{1... | collective-permute-start | bytes 393224 | tf_op jit(solution)/shard_map/ppermute | solution.py:13
  241.0 1.3 copy-start.2
  241.2 13.5 %copy-start.1 = (f32[128,256]{1,0:T(8,128)S(1)}, f32[128,256]{1,0:T(8,128)}, u32[]{:S(2)}) copy-start(f32[128,256]{1,0:T(8,128)} %reduce-scatter.3.cloned.1.call-done) | copy-start | bytes 393220
Sparse Core Ops, SparseCore 0:
  210.7 6.7 reduce-scatter.2
  243.4 11.2 reduce-scatter.4
where the time goes:
time: 264 us; the launch traced here: 263 us
  waiting for transfers between devices  156 us (59%)
  other arithmetic  32.1 us (12%)
  starting transfers between devices  19.5 us (7%)
  local copies, waits for them, and re-layouts  18.7 us (7%)
  between operations  17.1 us (6%)
  matrix products  12.8 us (5%)
  blocking collectives  7.4 us (3%)
    all_to_all x1, waiting for transfers between devices, body(): lax.all_to_all(packed, 'tiles', split_axis=0, concat_axis=0, tiled=True)  133 us
    scatter x1, other arithmetic, bucket_rows(): jnp.zeros((buckets * capacity, width), hidden.dtype).at[slot_of].set(hidden)  23.1 us
    scatter x1, local copies, waits for them, and re-layouts, bucket_rows(): jnp.full((buckets * capacity,), -1, jnp.int32).at[slot_of].set(local_id)  16.3 us
    reduce_scatter x1, waiting for transfers between devices, body(): lax.psum_scatter(partial_out, 'feat', scatter_dimension=1, tiled=True)  11.5 us
    ppermute x4, waiting for transfers between devices, from_behind(): return lax.ppermute(block, axis, route)  8.67 us
    ppermute x4, starting transfers between devices, from_behind(): return lax.ppermute(block, axis, route)  7.57 us
    all_to_all x1, starting transfers between devices, body(): lax.all_to_all(labels, 'tiles', split_axis=0, concat_axis=0, tiled=True)  6.32 us
    dot_general x1, matrix products, body(): jnp.dot(points, w_point, preferred_element_type=jnp.float32)  5.39 us
  transfers between devices with their start and end apart: 8, of which 5 were waited for; matrix products, arithmetic and copies ran while one was open for 12% of the time, Pallas kernels for 0%

commit v1 on v0

v1 whole, which is shorter than its diff:
```python
import functools

import jax
import jax.numpy as jnp
from jax import lax
from jax.experimental import pallas as pl
from jax.experimental.pallas import tpu as pltpu
from jax.sharding import PartitionSpec as P

S_BLK = 128
REACH = 2
HEAD = 64
CHUNK = 1024
MESH = pl.DeviceIdType.MESH
OFFSETS = tuple(range(-REACH, 0)) + tuple(range(1, REACH + 1))
NT = (((1,), (1,)), ((), ()))
F32 = jnp.float32
BF16 = jnp.bfloat16


def loop(count, step):
    if count <= 8:
        for k in range(count):
            step(k)
    else:
        lax.fori_loop(0, count, lambda k, c: (step(k), c)[1], 0)


def kernel(
    T, R, F, H,
    dest_ref, member_ref, temper_ref, adj_ref, gain_ref, points_hbm, wp_hbm, wqkv_hbm, wo_hbm,
    out_ref,
    pts, wp, wqkv, wo, hid, moh, cnt_send, cnt_recv, tsum, rep_send, rep_recv, z_send, z_recv,
    pool, kv_own, kv_recv, att, qm, lsum, acc,
    in_sem, wo_ss, wo_rs, cnt_ss, cnt_rs, rep_ss, rep_rs, z_ss, z_rs, pool_ss, pool_rs,
    kv_ss, kv_rs, att_ss, att_rs,
):
    t, r, f = lax.axis_index("tiles"), lax.axis_index("rep"), lax.axis_index("feat")
    other = 1 - r
    rows = pts.shape[0]
    dim = pts.shape[1]
    wid = wp.shape[1]
    chunks = rows // CHUNK
    blocks = T * R
    block = t * R + r

    loads = [pltpu.make_async_copy(wp_hbm, wp, in_sem.at[chunks])]
    for c in range(chunks):
        part = pl.ds(c * CHUNK, CHUNK)
        loads.append(pltpu.make_async_copy(points_hbm.at[part], pts.at[part], in_sem.at[c]))
    loads.append(pltpu.make_async_copy(wqkv_hbm, wqkv, in_sem.at[chunks + 1]))
    my_cols = pl.ds(pl.multiple_of(f * wid, 128), wid)
    loads.append(pltpu.make_async_copy(wo_hbm.at[:, my_cols], wo.at[f], in_sem.at[chunks + 2]))
    for load in loads:
        load.start()

    barrier = pltpu.get_barrier_semaphore()

    def greet(i):
        pl.semaphore_signal(
            barrier, inc=1, device_id={"tiles": lax.rem(t + i, T), "rep": r}, device_id_type=MESH
        )
        pl.semaphore_signal(
            barrier, inc=1, device_id={"tiles": lax.rem(t + i, T), "rep": other},
            device_id_type=MESH,
        )

    loop(T - 1, lambda k: greet(k + 1))
    pl.semaphore_signal(barrier, inc=1, device_id={"rep": other}, device_id_type=MESH)
    for i in range(1, F):
        pl.semaphore_signal(
            barrier, inc=1, device_id={"feat": lax.rem(f + i, F)}, device_id_type=MESH
        )

    t_rows = max(T, 16)
    counts = jnp.zeros((t_rows, R * S_BLK), F32)
    for c in range(chunks):
        cols = pl.ds(c * CHUNK, CHUNK)
        ids = lax.broadcasted_iota(jnp.int32, (R * S_BLK, CHUNK), 0)
        hot = jnp.where(ids == member_ref[:, cols], 1.0, 0.0).astype(BF16)
        moh[:, cols] = hot
        tids = lax.broadcasted_iota(jnp.int32, (t_rows, CHUNK), 0)
        thot = jnp.where(tids == dest_ref[:, cols], 1.0, 0.0).astype(BF16)
        counts += lax.dot_general(thot, hot, NT, preferred_element_type=F32)
    for i in range(T):
        for j in range(R):
            cnt_send[i, j] = jnp.broadcast_to(
                counts[i : i + 1, j * S_BLK : (j + 1) * S_BLK], (8, S_BLK)
            )

    pl.semaphore_wait(barrier, R * T - 1 + F - 1)

    def remote(src, dst, ss, rs, device):
        return pltpu.make_async_remote_copy(
            src_ref=src, dst_ref=dst, send_sem=ss, recv_sem=rs, device_id=device,
            device_id_type=MESH,
        )

    def wo_copy(i):
        p = lax.rem(f + i, F)
        cols = pl.ds(pl.multiple_of(p * wid, 128), wid)
        return remote(wo_hbm.at[:, cols], wo.at[f], wo_ss.at[p], wo_rs.at[f], {"feat": p})

    def cnt_copy(i, j):
        p = lax.rem(t + i, T)
        return remote(
            cnt_send.at[p, j], cnt_recv.at[t, r], cnt_ss.at[p, j], cnt_rs.at[t, r],
            {"tiles": p, "rep": j},
        )

    loop(T - 1, lambda k: (cnt_copy(k + 1, r).start(), cnt_copy(k + 1, other).start()))
    cnt_copy(0, other).start()
    for i in range(1, F):
        wo_copy(i).start()

    loads[0].wait()
    for c in range(chunks):
        loads[1 + c].wait()
        part = pl.ds(c * CHUNK, CHUNK)
        x = jnp.dot(pts[part], wp[...], preferred_element_type=F32)
        inner = 0.7978845608028654 * (x + 0.044715 * (x * x * x))
        hid[part] = (0.5 * x * (1.0 + jnp.tanh(inner))).astype(BF16)

    def tile_at(k):
        return lax.rem(t + 1 + lax.rem(T // 2 - 1 - k + (T - 1), T - 1), T)

    def rep_copy(k):
        return remote(
            rep_send.at[k], rep_recv.at[k], rep_ss.at[k], rep_rs.at[k], {"rep": other}
        )

    def z_copy(k):
        return remote(
            z_send.at[k], z_recv.at[t], z_ss.at[k], z_rs.at[t], {"tiles": tile_at(k)}
        )

    def sum_tile(k, tile):
        here = jnp.where(dest_ref[...] == tile, 1.0, 0.0).astype(BF16)
        sums = jnp.dot(moh[...] * here, hid[...], preferred_element_type=F32)
        for j in range(R):
            tsum[k, j] = sums[j * S_BLK : (j + 1) * S_BLK]
        rep_send[k] = tsum[k, other].astype(BF16)
        rep_copy(k).start()

    def pass_on(k):
        rep_copy(k).wait_recv()
        z_send[k] = (tsum[k, r] + rep_recv[k].astype(F32)).astype(BF16)
        z_copy(k).start()

    sum_tile(0, tile_at(0))

    def middle(k):
        sum_tile(k + 1, tile_at(k + 1))
        pass_on(k)

    loop(T - 2, middle)
    sum_tile(T - 1, t)
    pass_on(T - 2)

    cnt_recv[t, r] = cnt_send[t, r]

    def cnt_wait(i, j):
        p = lax.rem(t + i, T)
        remote(
            cnt_send.at[p, j], cnt_recv.at[p, j], cnt_ss.at[p, j], cnt_rs.at[p, j],
            {"tiles": p, "rep": j},
        ).wait_recv()

    loop(T - 1, lambda k: (cnt_wait(k + 1, r), cnt_wait(k + 1, other)))
    cnt_wait(0, other)
    total = jnp.sum(cnt_recv[...].reshape(blocks, 8, S_BLK), axis=0)
    column = jnp.transpose(jnp.broadcast_to(total[0:1], (S_BLK, S_BLK)))
    column = jnp.maximum(column, 1.0)

    rep_copy(T - 1).wait_recv()
    tsum[T - 1, r] += rep_recv[T - 1].astype(F32)

    def gather_sum(i):
        p = lax.rem(t + i, T)
        remote(z_send.at[0], z_recv.at[p], z_ss.at[0], z_rs.at[p], {"tiles": p}).wait_recv()
        tsum[T - 1, r] += z_recv[p].astype(F32)

    loop(T - 1, lambda k: gather_sum(k + 1))
    sums = tsum[T - 1, r]
    pooled = jnp.concatenate(
        [sums[:, g * 128 : (g + 1) * 128] / column for g in range(wid // 128)], axis=1
    ).astype(BF16)
    pool[f] = pooled

    def feat_copy(ref, ss, rs, i):
        p = lax.rem(f + i, F)
        return remote(ref.at[f], ref.at[f], ss.at[p], rs.at[f], {"feat": p})

    def feat_wait(ref, ss, rs, i):
        p = lax.rem(f + i, F)
        remote(ref.at[p], ref.at[p], ss.at[p], rs.at[p], {"feat": p}).wait_recv()

    for i in range(1, F):
        feat_copy(pool, pool_ss, pool_rs, i).start()
    loads[chunks + 1].wait()
    for i in range(1, F):
        feat_wait(pool, pool_ss, pool_rs, i)

    lifted = jnp.concatenate([pool[p].astype(F32) for p in range(F)], axis=1)
    mean = jnp.sum(lifted, axis=1, keepdims=True) * (1.0 / dim)
    centred = lifted - mean
    var = jnp.sum(centred * centred, axis=1, keepdims=True) * (1.0 / dim)
    normed = (centred * lax.rsqrt(var + 1e-05) * gain_ref[...]).astype(BF16)

    same_head = (
        lax.broadcasted_iota(jnp.int32, (wid, wid), 0) // HEAD
        == lax.broadcasted_iota(jnp.int32, (wid, wid), 1) // HEAD
    )
    spread = jnp.where(same_head, 1.0, 0.0).astype(BF16)

    def project(i):
        return jnp.dot(normed, wqkv[i], preferred_element_type=F32)

    def unit(proj):
        square = proj * proj
        high = square.astype(BF16)
        low = (square - high.astype(F32)).astype(BF16)
        norm = jnp.dot(high, spread, preferred_element_type=F32) + jnp.dot(
            low, spread, preferred_element_type=F32
        )
        return (proj * lax.rsqrt(norm + 1e-06)).astype(BF16)

    def inside(offset):
        return (block + offset >= 0) & (block + offset < blocks)

    def kv_copy(i, j):
        slot = len(OFFSETS) - 1 - j
        goal = block + OFFSETS[j]
        return remote(
            kv_own.at[i], kv_recv.at[slot, i], kv_ss.at[j, i], kv_rs.at[slot, i],
            {"tiles": goal // R, "rep": lax.rem(goal, R)},
        )

    def kv_wait(i, j):
        goal = block + OFFSETS[j]
        remote(
            kv_own.at[i], kv_recv.at[j, i], kv_ss.at[j, i], kv_rs.at[j, i],
            {"tiles": goal // R, "rep": lax.rem(goal, R)},
        ).wait_recv()

    def send_kv(i):
        for j in (0, len(OFFSETS) - 1, 1, 2):
            @pl.when(inside(OFFSETS[j]))
            def _():
                kv_copy(i, j).start()

    kv_own[0] = unit(project(1))
    send_kv(0)
    kv_own[1] = project(2).astype(BF16)
    send_kv(1)
    query = unit(project(0))
    lane_head = lax.broadcasted_iota(jnp.int32, (S_BLK, wid), 1) // HEAD
    for h in range(H):
        qm[h * S_BLK : (h + 1) * S_BLK] = jnp.where(lane_head == h, query, jnp.zeros_like(query))

    def attend(keys, values, mask, first):
        scores = lax.dot_general(qm[...], keys, NT, preferred_element_type=F32)
        expd = jnp.concatenate(
            [
                jnp.exp(scores[h * S_BLK : (h + 1) * S_BLK] * temper_ref[h])
                for h in range(H)
            ],
            axis=0,
        )
        if mask is not None:
            expd = expd * mask
        got = jnp.dot(expd.astype(BF16), values, preferred_element_type=F32)
        if first:
            lsum[...] = expd
            acc[...] = got
        else:
            lsum[...] += expd
            acc[...] += got

    attend(kv_own[0], kv_own[1], None, True)
    for j in (1, 2, 0, 3):
        @pl.when(inside(OFFSETS[j]))
        def _():
            kv_wait(0, j)
            kv_wait(1, j)
            mask = jnp.where(adj_ref[0, j] == 1, 1.0, 0.0).astype(F32)
            attend(kv_recv[j, 0], kv_recv[j, 1], mask, False)

    attended = jnp.zeros((S_BLK, wid), F32)
    for h in range(H):
        part = slice(h * S_BLK, (h + 1) * S_BLK)
        scale = 1.0 / jnp.sum(lsum[part], axis=1, keepdims=True)
        attended = jnp.where(lane_head == h, acc[part] * scale, attended)
    att[f] = attended.astype(BF16)
    for i in range(1, F):
        feat_copy(att, att_ss, att_rs, i).start()
    loads[chunks + 2].wait()
    mixed = pool[f].astype(F32) + jnp.dot(att[f], wo[f], preferred_element_type=F32)
    for i in range(1, F):
        p = lax.rem(f + i, F)
        remote(wo.at[p], wo.at[p], wo_ss.at[p], wo_rs.at[p], {"feat": p}).wait_recv()
        feat_wait(att, att_ss, att_rs, i)
        mixed += jnp.dot(att[p], wo[p], preferred_element_type=F32)
    out_ref[...] = mixed.astype(out_ref.dtype)

    loop(T - 1, lambda k: (cnt_copy(k + 1, r).wait_send(), cnt_copy(k + 1, other).wait_send()))
    cnt_copy(0, other).wait_send()
    loop(T, lambda k: rep_copy(k).wait_send())
    loop(T - 1, lambda k: z_copy(k).wait_send())
    for i in range(1, F):
        wo_copy(i).wait_send()
        feat_copy(pool, pool_ss, pool_rs, i).wait_send()
        feat_copy(att, att_ss, att_rs, i).wait_send()
    for j in range(len(OFFSETS)):
        @pl.when(inside(OFFSETS[j]))
        def _():
            kv_copy(0, j).wait_send()
            kv_copy(1, j).wait_send()


def body(points, dest_tile, member, w_point, ln_gain, w_qkv, temper, w_out, adjacency):
    T, R, F = lax.axis_size("tiles"), lax.axis_size("rep"), lax.axis_size("feat")
    H = temper.shape[0]
    rows, dim = points.shape
    wid = w_point.shape[1]
    near = len(OFFSETS)
    vmem = pl.BlockSpec(memory_space=pltpu.VMEM)
    smem = pl.BlockSpec(memory_space=pltpu.SMEM)
    anyw = pl.BlockSpec(memory_space=pl.ANY)
    dma = pltpu.SemaphoreType.DMA
    return pl.pallas_call(
        functools.partial(kernel, T, R, F, H),
        out_shape=jax.ShapeDtypeStruct((S_BLK, wid), BF16),
        in_specs=[vmem, vmem, smem, smem, vmem, anyw, anyw, anyw, anyw],
        out_specs=vmem,
        scratch_shapes=[
            pltpu.VMEM((rows, dim), BF16),
            pltpu.VMEM((dim, wid), BF16),
            pltpu.VMEM((3, dim, wid), BF16),
            pltpu.VMEM((F, wid, wid), BF16),
            pltpu.VMEM((rows, wid), BF16),
            pltpu.VMEM((R * S_BLK, rows), BF16),
            pltpu.VMEM((T, R, 8, S_BLK), F32),
            pltpu.VMEM((T, R, 8, S_BLK), F32),
            pltpu.VMEM((T, R, S_BLK, wid), F32),
            pltpu.VMEM((T, S_BLK, wid), BF16),
            pltpu.VMEM((T, S_BLK, wid), BF16),
            pltpu.VMEM((T, S_BLK, wid), BF16),
            pltpu.VMEM((T, S_BLK, wid), BF16),
            pltpu.VMEM((F, S_BLK, wid), BF16),
            pltpu.VMEM((2, S_BLK, wid), BF16),
            pltpu.VMEM((near, 2, S_BLK, wid), BF16),
            pltpu.VMEM((F, S_BLK, wid), BF16),
            pltpu.VMEM((H * S_BLK, wid), BF16),
            pltpu.VMEM((H * S_BLK, S_BLK), F32),
            pltpu.VMEM((H * S_BLK, wid), F32),
            dma((rows // CHUNK + 3,)),
            dma((F,)), dma((F,)),
            dma((T, R)), dma((T, R)),
            dma((T,)), dma((T,)),
            dma((T,)), dma((T,)),
            dma((F,)), dma((F,)),
            dma((near, 2)), dma((near, 2)),
            dma((F,)), dma((F,)),
        ],
        compiler_params=pltpu.CompilerParams(
            collective_id=0, has_side_effects=True, vmem_limit_bytes=48 * 1024 * 1024
        ),
    )(
        dest_tile.reshape(1, rows), member.reshape(1, rows), temper, adjacency,
        ln_gain.reshape(1, dim), points, w_point, w_qkv, w_out,
    )


def solution(mesh):
    return jax.shard_map(
        body,
        mesh=mesh,
        in_specs=(
            P(("groups", "tiles", "rep"), None),
            P(("groups", "tiles", "rep"), None),
            P(("groups", "tiles", "rep")),
            P(None, "feat"),
            P(),
            P(None, None, "feat"),
            P("feat"),
            P("feat", None),
            P(("groups", "tiles", "rep"), None),
        ),
        out_specs=P(("groups", "tiles", "rep"), "feat"),
        check_vma=False,
    )
```

time: 264 us -> 41 us (0.16)
  waiting for transfers between devices: 156 us -> 0 us
  other arithmetic: 32.1 us -> 0 us
  Pallas kernels: 0 us -> 31 us
  starting transfers between devices: 19.5 us -> 0 us
  between operations: 17.1 us -> 0.02 us
  matrix products: 12.8 us -> 0 us
  local copies, waits for them, and re-layouts: 18.7 us -> 9.28 us
  blocking collectives: 7.4 us -> 0 us
    all_to_all x2 -> x0, waiting for transfers between devices: 133 us -> none  [the longest x1 133 us: body(): lax.all_to_all(packed, 'tiles', split_axis=0, concat_axis=0, tiled=True)]
    pallas_call x0 -> x1, Pallas kernels: none -> 31 us  [body(): pl.pallas_call(functools.partial(kernel, T, R, F, H), out_shape=jax.Shape...]
    scatter x1 -> x0, other arithmetic: 23.1 us -> none  [bucket_rows(): jnp.zeros((buckets * capacity, width), hidden.dtype).at[slot_of].set(hidden)]
    scatter x1 -> x0, local copies, waits for them, and re-layouts: 16.3 us -> none  [bucket_rows(): jnp.full((buckets * capacity,), -1, jnp.int32).at[slot_of].set(local_id)]
    reduce_scatter x2 -> x0, waiting for transfers between devices: 13.5 us -> none  [the longest x1 11.5 us: body(): lax.psum_scatter(partial_out, 'feat', scatter_dimension=1, tiled=True)]
    dot_general x6 -> x0, matrix products: 12.8 us -> none  [the longest x1 5.39 us: body(): jnp.dot(points, w_point, preferred_element_type=jnp.float32)]
    all_to_all x2 -> x0, starting transfers between devices: 11.7 us -> none  [the longest x1 6.32 us: body(): lax.all_to_all(labels, 'tiles', split_axis=0, concat_axis=0, tiled=True)]
    ppermute x4 -> x0, waiting for transfers between devices: 8.67 us -> none  [from_behind(): return lax.ppermute(block, axis, route)]
  transfers between devices with their start and end apart: 8 -> 0, of which waited for: 5 -> 0; matrix products, arithmetic and copies ran while one was open for 12% -> 0% of each run, Pallas kernels for 0% -> 0%
where the time goes in v1:
time: 41 us; the launch traced here: 40.3 us
  Pallas kernels  31 us (76%)
  local copies, waits for them, and re-layouts  9.28 us (23%)
    pallas_call x1, Pallas kernels, body(): pl.pallas_call(functools.partial(kernel, T, R, F, H), out_shape=jax.Shape...  31 us
    unnamed x19, local copies, waits for them, and re-layouts  9.28 us

profile of v1, /device:TPU:0, one launch (start us, length us, event | category | flops | bytes accessed | tf_op | source)
XLA Modules:
  0.0 40.3 jit_solution(13160664126881195523)
XLA Ops:
  0.0 0.0 copy-start
  0.0 2.2 %copy-done = bf16[4096,512]{1,0:T(8,128)(2,1)S(1)} copy-done((bf16[4096,512]{1,0:T(8,128)(2,1)S(1)}, bf16[4096,512]{1,0:T(8,128)(2,1)}, u32[]{:S(2)}) %copy-start) | copy-done | bytes 4194328
  2.2 0.0 copy-start.1
  2.2 1.1 %copy-done.1 = bf16[3,512,256]{2,1,0:T(8,128)(2,1)S(1)} copy-done((bf16[3,512,256]{2,1,0:T(8,128)(2,1)S(1)}, bf16[3,512,256]{2,1,0:T(8,128)(2,1)}, u32[]{:S(2)}) %copy-start.1) | copy-done | bytes 786456
  3.3 0.0 copy-start.2
  3.3 0.9 %copy-done.2 = bf16[512,256]{1,0:T(8,128)(2,1)S(1)} copy-done((bf16[512,256]{1,0:T(8,128)(2,1)S(1)}, bf16[512,256]{1,0:T(8,128)(2,1)}, u32[]{:S(2)}) %copy-start.2) | copy-done | bytes 262168
  4.3 0.0 copy-start.3
  4.3 0.9 %copy-done.3 = bf16[256,512]{1,0:T(8,128)(2,1)S(1)} copy-done((bf16[256,512]{1,0:T(8,128)(2,1)S(1)}, bf16[256,512]{1,0:T(8,128)(2,1)}, u32[]{:S(2)}) %copy-start.3) | copy-done | bytes 262168
  5.2 0.0 copy-start.4
  5.2 0.7 %copy-done.4 = s32[4096,1]{0,1:T(1,128)S(1)} copy-done((s32[4096,1]{0,1:T(1,128)S(1)}, s32[4096,1]{0,1:T(1,128)}, u32[]{:S(2)}) %copy-start.4) | copy-done | bytes 16408
  5.9 0.0 copy-start.5
  5.9 0.7 %copy-done.5 = s32[4096]{0:T(1024)S(1)} copy-done((s32[4096]{0:T(1024)S(1)}, s32[4096]{0:T(1024)}, u32[]{:S(2)}) %copy-start.5) | copy-done | bytes 16408
  6.7 0.0 copy-start.6
  6.7 0.7 %copy-done.6 = f32[512]{0:T(512)S(1)} copy-done((f32[512]{0:T(512)S(1)}, f32[512]{0:T(512)}, u32[]{:S(2)}) %copy-start.6) | copy-done | bytes 2072
  7.3 0.0 copy-start.7
  7.3 0.7 %copy-done.7 = f32[4]{0:T(128)S(1)} copy-done((f32[4]{0:T(128)S(1)}, f32[4]{0:T(128)}, u32[]{:S(2)}) %copy-start.7) | copy-done | bytes 40
  8.0 0.0 copy-start.8
  8.0 0.7 %copy-done.8 = s32[1,4]{1,0:T(1,128)S(1)} copy-done((s32[1,4]{1,0:T(1,128)S(1)}, s32[1,4]{1,0:T(1,128)}, u32[]{:S(2)}) %copy-start.8) | copy-done | bytes 40
  8.7 31.0 %shard_map.91 = bf16[128,256]{1,0:T(8,128)(2,1)S(1)} custom-call(s32[1,4096]{1,0:T(1,128)S(1)} %bitcast.3, s32[1,4096]{1,0:T(1,128)S(1)} %bitcast.4, f32[4]{0:T(128)S(1)} %copy-done.7, s32[1,4]{1,0:T(1,128)S(1)} %copy-done.8, f32[1,512]{1,0:T(1,128)S(1)} %bitcast.5, bf16[4096,512]{1,0:T(8,128)(2,1)S(1)} %copy-done, bf16[512,256]{1,0:T(8,128)(2,1)S(1)} %copy-done.2, ...), custom_call_target="tpu_custom_call" | custom-call | tf_op jit(solution)/shard_map/pallas_call | solution.py:331
  39.7 0.6 %copy.11 = bf16[128,256]{1,0:T(8,128)(2,1)} copy(bf16[128,256]{1,0:T(8,128)(2,1)S(1)} %shard_map.91) | data formatting | bytes 131072
Async XLA Ops:
  0.0 2.2 %copy-start = (bf16[4096,512]{1,0:T(8,128)(2,1)S(1)}, bf16[4096,512]{1,0:T(8,128)(2,1)}, u32[]{:S(2)}) copy-start(bf16[4096,512]{1,0:T(8,128)(2,1)} %points_hbm.1) | copy-start | bytes 12582916
  2.2 1.1 %copy-start.1 = (bf16[3,512,256]{2,1,0:T(8,128)(2,1)S(1)}, bf16[3,512,256]{2,1,0:T(8,128)(2,1)}, u32[]{:S(2)}) copy-start(bf16[3,512,256]{2,1,0:T(8,128)(2,1)} %wqkv_hbm.1) | copy-start | bytes 2359300
  3.3 0.9 %copy-start.2 = (bf16[512,256]{1,0:T(8,128)(2,1)S(1)}, bf16[512,256]{1,0:T(8,128)(2,1)}, u32[]{:S(2)}) copy-start(bf16[512,256]{1,0:T(8,128)(2,1)} %wp_hbm.1) | copy-start | bytes 786436
  4.3 0.9 %copy-start.3 = (bf16[256,512]{1,0:T(8,128)(2,1)S(1)}, bf16[256,512]{1,0:T(8,128)(2,1)}, u32[]{:S(2)}) copy-start(bf16[256,512]{1,0:T(8,128)(2,1)} %wo_hbm.1) | copy-start | bytes 786436
  5.2 0.7 %copy-start.4 = (s32[4096,1]{0,1:T(1,128)S(1)}, s32[4096,1]{0,1:T(1,128)}, u32[]{:S(2)}) copy-start(s32[4096,1]{0,1:T(1,128)} %param.10) | copy-start | bytes 49156
  5.9 0.7 %copy-start.5 = (s32[4096]{0:T(1024)S(1)}, s32[4096]{0:T(1024)}, u32[]{:S(2)}) copy-start(s32[4096]{0:T(1024)} %param.11) | copy-start | bytes 49156
  6.7 0.7 %copy-start.6 = (f32[512]{0:T(512)S(1)}, f32[512]{0:T(512)}, u32[]{:S(2)}) copy-start(f32[512]{0:T(512)} %param.13) | copy-start | bytes 6148
  7.3 0.7 %copy-start.7 = (f32[4]{0:T(128)S(1)}, f32[4]{0:T(128)}, u32[]{:S(2)}) copy-start(f32[4]{0:T(128)} %temper_ref.1) | copy-start | bytes 52
  8.0 0.7 %copy-start.8 = (s32[1,4]{1,0:T(1,128)S(1)}, s32[1,4]{1,0:T(1,128)}, u32[]{:S(2)}) copy-start(s32[1,4]{1,0:T(1,128)} %adj_ref.1) | copy-start | bytes 52

commit v2 on v1

--- a/solution.py
+++ b/solution.py
@@ -28,9 +28,9 @@
 
 def kernel(
     T, R, F, H,
-    dest_ref, member_ref, temper_ref, adj_ref, gain_ref, points_hbm, wp_hbm, wqkv_hbm, wo_hbm,
+    dest_hbm, member_hbm, temper_hbm, adj_hbm, gain_hbm, points_hbm, wp_hbm, wqkv_hbm, wo_hbm,
     out_ref,
-    pts, wp, wqkv, wo, hid, moh, cnt_send, cnt_recv, tsum, rep_send, rep_recv, z_send, z_recv,
+    dest_ref, member_ref, temper_ref, adj_ref, gain_ref, pts, wp, wqkv, wo, hid, moh, cnt_send, cnt_recv, tsum, rep_send, rep_recv, z_send, z_recv,
     pool, kv_own, kv_recv, att, qm, lsum, acc,
     in_sem, wo_ss, wo_rs, cnt_ss, cnt_rs, rep_ss, rep_rs, z_ss, z_rs, pool_ss, pool_rs,
     kv_ss, kv_rs, att_ss, att_rs,
@@ -51,7 +51,16 @@
     loads.append(pltpu.make_async_copy(wqkv_hbm, wqkv, in_sem.at[chunks + 1]))
     my_cols = pl.ds(pl.multiple_of(f * wid, 128), wid)
     loads.append(pltpu.make_async_copy(wo_hbm.at[:, my_cols], wo.at[f], in_sem.at[chunks + 2]))
-    for load in loads:
+    ids_in = [
+        pltpu.make_async_copy(member_hbm, member_ref, in_sem.at[chunks + 3]),
+        pltpu.make_async_copy(dest_hbm, dest_ref, in_sem.at[chunks + 4]),
+    ]
+    small = [
+        pltpu.make_async_copy(temper_hbm, temper_ref, in_sem.at[chunks + 5]),
+        pltpu.make_async_copy(adj_hbm, adj_ref, in_sem.at[chunks + 6]),
+        pltpu.make_async_copy(gain_hbm, gain_ref, in_sem.at[chunks + 7]),
+    ]
+    for load in ids_in + loads + small:
         load.start()
 
     barrier = pltpu.get_barrier_semaphore()
@@ -71,6 +80,9 @@
         pl.semaphore_signal(
             barrier, inc=1, device_id={"feat": lax.rem(f + i, F)}, device_id_type=MESH
         )
+
+    for load in ids_in:
+        load.wait()
 
     t_rows = max(T, 16)
     counts = jnp.zeros((t_rows, R * S_BLK), F32)
@@ -198,6 +210,8 @@
     for i in range(1, F):
         feat_copy(pool, pool_ss, pool_rs, i).start()
     loads[chunks + 1].wait()
+    for load in small:
+        load.wait()
     for i in range(1, F):
         feat_wait(pool, pool_ss, pool_rs, i)
 
@@ -254,6 +268,7 @@
     kv_own[1] = project(2).astype(BF16)
     send_kv(1)
     query = unit(project(0))
+    temper = temper_ref[...]
     lane_head = lax.broadcasted_iota(jnp.int32, (S_BLK, wid), 1) // HEAD
     for h in range(H):
         qm[h * S_BLK : (h + 1) * S_BLK] = jnp.where(lane_head == h, query, jnp.zeros_like(query))
@@ -262,7 +277,7 @@
         scores = lax.dot_general(qm[...], keys, NT, preferred_element_type=F32)
         expd = jnp.concatenate(
             [
-                jnp.exp(scores[h * S_BLK : (h + 1) * S_BLK] * temper_ref[h])
+                jnp.exp(scores[h * S_BLK : (h + 1) * S_BLK] * temper[:, h : h + 1])
                 for h in range(H)
             ],
             axis=0,
@@ -283,7 +298,7 @@
         def _():
             kv_wait(0, j)
             kv_wait(1, j)
-            mask = jnp.where(adj_ref[0, j] == 1, 1.0, 0.0).astype(F32)
+            mask = jnp.where(adj_ref[:, j : j + 1] == 1, 1.0, 0.0).astype(F32)
             attend(kv_recv[j, 0], kv_recv[j, 1], mask, False)
 
     attended = jnp.zeros((S_BLK, wid), F32)
@@ -325,15 +340,19 @@
     wid = w_point.shape[1]
     near = len(OFFSETS)
     vmem = pl.BlockSpec(memory_space=pltpu.VMEM)
-    smem = pl.BlockSpec(memory_space=pltpu.SMEM)
-    anyw = pl.BlockSpec(memory_space=pl.ANY)
+    hbm = pl.BlockSpec(memory_space=pl.ANY)
     dma = pltpu.SemaphoreType.DMA
     return pl.pallas_call(
         functools.partial(kernel, T, R, F, H),
         out_shape=jax.ShapeDtypeStruct((S_BLK, wid), BF16),
-        in_specs=[vmem, vmem, smem, smem, vmem, anyw, anyw, anyw, anyw],
+        in_specs=[hbm] * 9,
         out_specs=vmem,
         scratch_shapes=[
+            pltpu.VMEM((1, rows), jnp.int32),
+            pltpu.VMEM((1, rows), jnp.int32),
+            pltpu.VMEM((1, H), F32),
+            pltpu.VMEM(adjacency.shape, jnp.int32),
+            pltpu.VMEM((1, dim), F32),
             pltpu.VMEM((rows, dim), BF16),
             pltpu.VMEM((dim, wid), BF16),
             pltpu.VMEM((3, dim, wid), BF16),
@@ -354,7 +373,7 @@
             pltpu.VMEM((H * S_BLK, wid), BF16),
             pltpu.VMEM((H * S_BLK, S_BLK), F32),
             pltpu.VMEM((H * S_BLK, wid), F32),
-            dma((rows // CHUNK + 3,)),
+            dma((rows // CHUNK + 8,)),
             dma((F,)), dma((F,)),
             dma((T, R)), dma((T, R)),
             dma((T,)), dma((T,)),
@@ -364,10 +383,10 @@
             dma((F,)), dma((F,)),
         ],
         compiler_params=pltpu.CompilerParams(
-            collective_id=0, has_side_effects=True, vmem_limit_bytes=48 * 1024 * 1024
+            collective_id=0, has_side_effects=True, vmem_limit_bytes=56000 * 1024
         ),
     )(
-        dest_tile.reshape(1, rows), member.reshape(1, rows), temper, adjacency,
+        dest_tile.reshape(1, rows), member.reshape(1, rows), temper.reshape(1, H), adjacency,
         ln_gain.reshape(1, dim), points, w_point, w_qkv, w_out,
     )
 

time: 41 us -> 32.7 us (0.80); the launches traced: 40.3 us -> 32.5 us
  local copies, waits for them, and re-layouts: 9.28 us -> 1.47 us
    unnamed x19 -> x1, local copies, waits for them, and re-layouts: 9.28 us -> 1.47 us
where the time goes in v2:
time: 32.7 us; the launch traced here: 32.5 us
  Pallas kernels  31 us (95%)
  local copies, waits for them, and re-layouts  1.47 us (4%)
    pallas_call x1, Pallas kernels, body(): pl.pallas_call(functools.partial(kernel, T, R, F, H), out_shape=jax.Shape...  31 us
    unnamed x1, local copies, waits for them, and re-layouts  1.47 us

profile of v2, /device:TPU:0, one launch (start us, length us, event | category | flops | bytes accessed | tf_op | source)
XLA Modules:
  0.0 32.5 jit_solution(76065238758249668)
XLA Ops:
  0.0 31.0 %shard_map.91 = bf16[128,256]{1,0:T(8,128)(2,1)} custom-call(s32[1,4096]{1,0:T(1,128)} %bitcast.4, s32[1,4096]{1,0:T(1,128)} %bitcast.5, f32[1,4]{1,0:T(1,128)} %bitcast.7, s32[1,4]{1,0:T(1,128)} %adj_hbm.1, f32[1,512]{1,0:T(1,128)} %bitcast.6, bf16[4096,512]{1,0:T(8,128)(2,1)} %points_hbm.1, bf16[512,256]{1,0:T(8,128)(2,1)} %wp_hbm.1, ...), custom_call_target="tpu_custom_call" | custom-call | tf_op jit(solution)/shard_map/pallas_call | solution.py:345
  31.0 1.5 %copy.11 = bf16[128,256]{1,0:T(8,128)(2,1)} copy(bf16[128,256]{1,0:T(8,128)(2,1)} %shard_map.91) | data formatting | bytes 131072

commit v3 on v2

--- a/solution.py
+++ b/solution.py
@@ -242,26 +242,39 @@
     def inside(offset):
         return (block + offset >= 0) & (block + offset < blocks)
 
+    sib, cross, handed = 2 - r, 1 + r, 3 * (1 - r)
+    steps = {0: -1, 3: 1}
+
     def kv_copy(i, j):
         slot = len(OFFSETS) - 1 - j
-        goal = block + OFFSETS[j]
         return remote(
             kv_own.at[i], kv_recv.at[slot, i], kv_ss.at[j, i], kv_rs.at[slot, i],
-            {"tiles": goal // R, "rep": lax.rem(goal, R)},
+            {"tiles": t + steps[j]},
+        )
+
+    def sib_copy(i):
+        return remote(
+            kv_own.at[i], kv_recv.at[1 + r, i], kv_ss.at[sib, i], kv_rs.at[1 + r, i],
+            {"rep": other},
+        )
+
+    def hand_copy(i):
+        return remote(
+            kv_recv.at[handed, i], kv_recv.at[2 - r, i], kv_ss.at[cross, i],
+            kv_rs.at[2 - r, i], {"rep": other},
         )
 
     def kv_wait(i, j):
-        goal = block + OFFSETS[j]
         remote(
-            kv_own.at[i], kv_recv.at[j, i], kv_ss.at[j, i], kv_rs.at[j, i],
-            {"tiles": goal // R, "rep": lax.rem(goal, R)},
+            kv_own.at[i], kv_recv.at[j, i], kv_ss.at[j, i], kv_rs.at[j, i], {"rep": other}
         ).wait_recv()
 
     def send_kv(i):
-        for j in (0, len(OFFSETS) - 1, 1, 2):
+        for j in steps:
             @pl.when(inside(OFFSETS[j]))
             def _():
                 kv_copy(i, j).start()
+        sib_copy(i).start()
 
     kv_own[0] = unit(project(1))
     send_kv(0)
@@ -293,13 +306,35 @@
             acc[...] += got
 
     attend(kv_own[0], kv_own[1], None, True)
-    for j in (1, 2, 0, 3):
-        @pl.when(inside(OFFSETS[j]))
-        def _():
-            kv_wait(0, j)
-            kv_wait(1, j)
-            mask = jnp.where(adj_ref[:, j : j + 1] == 1, 1.0, 0.0).astype(F32)
-            attend(kv_recv[j, 0], kv_recv[j, 1], mask, False)
+
+    def take(j):
+        lanes = lax.broadcasted_iota(jnp.int32, adj_ref.shape, 1)
+        on = jnp.where((lanes == j) & (adj_ref[...] == 1), 1.0, 0.0)
+        mask = jnp.sum(on, axis=1, keepdims=True)
+        attend(kv_recv[j, 0], kv_recv[j, 1], mask, False)
+
+    kv_wait(0, sib)
+    kv_wait(1, sib)
+    take(sib)
+
+    @pl.when(inside(2 - 4 * r))
+    def _():
+        for i in range(2):
+            kv_wait(i, handed)
+            hand_copy(i).start()
+        take(handed)
+
+    @pl.when(inside(4 * r - 2))
+    def _():
+        kv_wait(0, 3 - handed)
+        kv_wait(1, 3 - handed)
+        take(3 - handed)
+
+    @pl.when(inside(2 * r - 1))
+    def _():
+        kv_wait(0, cross)
+        kv_wait(1, cross)
+        take(cross)
 
     attended = jnp.zeros((S_BLK, wid), F32)
     for h in range(H):
@@ -326,11 +361,18 @@
         wo_copy(i).wait_send()
         feat_copy(pool, pool_ss, pool_rs, i).wait_send()
         feat_copy(att, att_ss, att_rs, i).wait_send()
-    for j in range(len(OFFSETS)):
+    for i in range(2):
+        sib_copy(i).wait_send()
+    for j in steps:
         @pl.when(inside(OFFSETS[j]))
         def _():
             kv_copy(0, j).wait_send()
             kv_copy(1, j).wait_send()
+
+    @pl.when(inside(2 - 4 * r))
+    def _():
+        hand_copy(0).wait_send()
+        hand_copy(1).wait_send()
 
 
 def body(points, dest_tile, member, w_point, ln_gain, w_qkv, temper, w_out, adjacency):

time: 32.7 us -> 31.8 us (0.972)
  Pallas kernels: 31 us -> 30.1 us
    pallas_call x1, Pallas kernels: 31 us -> 30.1 us  [body(): pl.pallas_call(functools.partial(kernel, T, R, F, H), out_shape=jax.Shape...]
where the time goes in v3:
time: 31.8 us; the launch traced here: 31.6 us
  Pallas kernels  30.1 us (95%)
  local copies, waits for them, and re-layouts  1.47 us (5%)
    pallas_call x1, Pallas kernels, body(): pl.pallas_call(functools.partial(kernel, T, R, F, H), out_shape=jax.Shape...  30.1 us
    unnamed x1, local copies, waits for them, and re-layouts  1.47 us

profile of v3, /device:TPU:0, one launch (start us, length us, event | category | flops | bytes accessed | tf_op | source)
XLA Modules:
  0.0 31.6 jit_solution(13060539178489471796)
XLA Ops:
  0.0 30.1 %shard_map.91 = bf16[128,256]{1,0:T(8,128)(2,1)} custom-call(s32[1,4096]{1,0:T(1,128)} %bitcast.4, s32[1,4096]{1,0:T(1,128)} %bitcast.5, f32[1,4]{1,0:T(1,128)} %bitcast.7, s32[1,4]{1,0:T(1,128)} %adj_hbm.1, f32[1,512]{1,0:T(1,128)} %bitcast.6, bf16[4096,512]{1,0:T(8,128)(2,1)} %points_hbm.1, bf16[512,256]{1,0:T(8,128)(2,1)} %wp_hbm.1, ...), custom_call_target="tpu_custom_call" | custom-call | tf_op jit(solution)/shard_map/pallas_call | solution.py:387
  30.1 1.5 %copy.11 = bf16[128,256]{1,0:T(8,128)(2,1)} copy(bf16[128,256]{1,0:T(8,128)(2,1)} %shard_map.91) | data formatting | bytes 131072

commit v4 on v3

--- a/solution.py
+++ b/solution.py
@@ -10,7 +10,7 @@
 S_BLK = 128
 REACH = 2
 HEAD = 64
-CHUNK = 1024
+CHUNK = 2048
 MESH = pl.DeviceIdType.MESH
 OFFSETS = tuple(range(-REACH, 0)) + tuple(range(1, REACH + 1))
 NT = (((1,), (1,)), ((), ()))

time: 31.8 us -> 31.2 us (0.981)
  Pallas kernels: 30.1 us -> 29.5 us
    pallas_call x1, Pallas kernels: 30.1 us -> 29.5 us  [body(): pl.pallas_call(functools.partial(kernel, T, R, F, H), out_shape=jax.Shape...]
where the time goes in v4:
time: 31.2 us; the launch traced here: 31 us
  Pallas kernels  29.5 us (95%)
  local copies, waits for them, and re-layouts  1.47 us (5%)
    pallas_call x1, Pallas kernels, body(): pl.pallas_call(functools.partial(kernel, T, R, F, H), out_shape=jax.Shape...  29.5 us
    unnamed x1, local copies, waits for them, and re-layouts  1.47 us

profile of v4, /device:TPU:0, one launch (start us, length us, event | category | flops | bytes accessed | tf_op | source)
XLA Modules:
  0.0 31.0 jit_solution(8930248597683830631)
XLA Ops:
  0.0 29.5 %shard_map.91 = bf16[128,256]{1,0:T(8,128)(2,1)} custom-call(s32[1,4096]{1,0:T(1,128)} %bitcast.4, s32[1,4096]{1,0:T(1,128)} %bitcast.5, f32[1,4]{1,0:T(1,128)} %bitcast.7, s32[1,4]{1,0:T(1,128)} %adj_hbm.1, f32[1,512]{1,0:T(1,128)} %bitcast.6, bf16[4096,512]{1,0:T(8,128)(2,1)} %points_hbm.1, bf16[512,256]{1,0:T(8,128)(2,1)} %wp_hbm.1, ...), custom_call_target="tpu_custom_call" | custom-call | tf_op jit(solution)/shard_map/pallas_call | solution.py:387
  29.5 1.5 %copy.11 = bf16[128,256]{1,0:T(8,128)(2,1)} copy(bf16[128,256]{1,0:T(8,128)(2,1)} %shard_map.91) | data formatting | bytes 131072
